TPU v7x, 32 devices: a whole 2x2x4 slice. The times are simulated.
32 devices in a mesh: dp: 4 (over y, x), ctx: 8 (over z, core).
Axes of the slice: x: 2, y: 2, z: 4, core: 2. Of those that a mesh axis runs over, the one named last changes fastest.
Arguments:
- queries: bfloat16 [2048, 4096], P(('dp', 'ctx')), parts along dimension 0, may hold values from -6 to 6
- keys: bfloat16 [2048, 4096], P(('dp', 'ctx')), parts along dimension 0, may hold values from -6 to 6
- values: bfloat16 [2048, 4096], P(('dp', 'ctx')), parts along dimension 0, may hold values from -6 to 6
- doc_starts: int32 [2048], P(('dp', 'ctx')), parts along dimension 0, may hold values from 0 to 1
- decay_exps: int32 [32], replicated, may hold values from 1 to 2047
- norm_gain: float32 [4096], replicated, may hold values from 0.25 to 1.75
Outputs:
- attended: bfloat16 [2048, 4096], P(('dp', 'ctx')), parts along dimension 0
There are 4 independent parts, one for each index of `dp`. A program takes and returns all parts, laid end to end along the dimension named above; an argument that names none is the same for every part. Nothing has to cross between parts.
All inputs are finite; a program needn't handle non-finite values.
Results may differ from a plain program's by a relative error of at most 0.0053.
Values may be sent and summed in bfloat16 or wider, within the bound.
A program may use at most 192 MiB of HBM per device.

v0:
```python
import jax
import jax.numpy as jnp
from jax import lax
from jax.sharding import PartitionSpec as P

HEADS = 32
HEAD = 128


def prefix(value, axis, combine, identity):
    size, index = (lax.axis_size(axis), lax.axis_index(axis))
    everything = jax.tree.map(lambda part: lax.all_gather(part, axis), value)
    start = jax.tree.map(
        lambda part, zero: jnp.broadcast_to(jnp.asarray(zero, part.dtype), part.shape),
        value,
        identity,
    )

    def step(k, before):
        reached = k < index
        new = combine(before, jax.tree.map(lambda part: part[k], everything))
        return jax.tree.map(lambda a, b: jnp.where(reached, a, b), new, before)

    return lax.fori_loop(0, size, step, start)


def block_terms(qpart, key_portion, vpart, starts, decay_rate):
    segment_length = qpart.shape[0]
    count = jnp.cumsum(starts)
    token_position = jnp.arange(segment_length).astype(jnp.float32)
    same = (count[:, None] == count[None, :]) & (token_position[:, None] >= token_position[None, :])
    gaps = jnp.maximum(token_position[:, None] - token_position[None, :], 0.0)
    weight = jnp.where(same[None], jnp.exp(-decay_rate[:, None, None] * gaps[None]), 0.0)
    scores = jnp.einsum("ihd,jhd->hij", qpart, key_portion, preferred_element_type=jnp.float32)
    weighted = (scores * weight).astype(jnp.bfloat16)
    intra = jnp.einsum("hij,jhd->ihd", weighted, vpart, preferred_element_type=jnp.float32)
    fresh = (count == 0).astype(jnp.float32)
    qscale = jnp.exp(-decay_rate[None, :] * (token_position[:, None] + 1.0)) * fresh[:, None]
    trailing_part = (count == count[-1]).astype(jnp.float32)
    key_scale_factor = (
        jnp.exp(-decay_rate[None, :] * (segment_length - 1.0 - token_position[:, None]))
        * trailing_part[:, None]
    )
    key_decay_factor = (key_portion * key_scale_factor[:, :, None]).astype(jnp.bfloat16)
    state = jnp.einsum("jhd,jhe->hde", key_decay_factor, vpart, preferred_element_type=jnp.float32)
    factor = jnp.exp(-decay_rate * segment_length) * (count[-1] == 0).astype(jnp.float32)
    return (intra, qscale, state, factor)


def apply_carry(intra, qpart, qscale, carry):
    cross = jnp.einsum(
        "ihd,hde->ihe", qpart, carry.astype(jnp.bfloat16), preferred_element_type=jnp.float32
    )
    return intra + qscale[:, :, None] * cross


def head_norm(raw, gain):
    meansq = jnp.mean(raw * raw, axis=-1, keepdims=True)
    return (raw * lax.rsqrt(meansq + 1e-06) * gain).astype(jnp.bfloat16)


def chain_combine(earlier, later):
    return (later[1][:, None, None] * earlier[0] + later[0], earlier[1] * later[1])


def on_device(queries, keys, values, doc_starts, decay_exps, norm_gain):
    rows = queries.shape[0]
    decay_rate = decay_exps.astype(jnp.float32) / 65536.0
    gain = norm_gain.reshape(HEADS, HEAD)
    q_heads = queries.reshape(rows, HEADS, HEAD)
    k_heads = keys.reshape(rows, HEADS, HEAD)
    v_heads = values.reshape(rows, HEADS, HEAD)
    intra, qscale, state, factor = block_terms(q_heads, k_heads, v_heads, doc_starts, decay_rate)
    empty = (jnp.zeros((HEADS, HEAD, HEAD), jnp.float32), jnp.ones((HEADS,), jnp.float32))
    carried = prefix((state, factor), "ctx", chain_combine, empty)
    raw = apply_carry(intra, q_heads, qscale, carried[0])
    result = head_norm(raw, gain)
    return result.reshape(rows, HEADS * HEAD)


def solution(mesh):
    return jax.shard_map(
        on_device,
        mesh=mesh,
        in_specs=(
            P(("dp", "ctx"), None),
            P(("dp", "ctx"), None),
            P(("dp", "ctx"), None),
            P(("dp", "ctx")),
            P(),
            P(),
        ),
        out_specs=P(("dp", "ctx"), None),
        check_vma=False,
    )
```

profile of v0, /device:TPU:0, one launch (start us, length us, event | category | flops | bytes accessed | tf_op | source)
XLA Modules:
  0.0 198.4 jit_solution(14161728467324455688)
XLA Ops:
  6.5 0.0 copy-start
  6.5 0.0 all-gather.4.cloned.1.call-start
  6.5 0.8 copy.20
  7.3 0.1 broadcast_in_dim.18
  7.4 0.5 slice.6
  8.0 0.1 reduce
  8.7 0.6 compare_convert_fusion.1
  9.4 1.2 dynamic-slice
  11.3 0.7 multiply_negate_fusion
  12.1 0.1 exponential_multiply_fusion.1
  12.1 0.0 copy-done
  12.2 3.5 %fusion.8 = f32[32,128,128]{2,1,0:T(8,128)} fusion(f32[64,32]{0,1:T(8,128)S(1)} %get-tuple-element.129, bf16[64,4096]{1,0:T(8,128)(2,1)S(1)} %copy-done, bf16[64,4096]{1,0:T(8,128)(2,1)} %param.9), kind=kOutput, calls=%fused_computation.16 | convolution fusion | flops 67895296 | bytes 3153920 | tf_op jit(solution)/shard_map/jhd,jhe->hde/dot_general | solution.py:45
  15.7 0.0 all-gather.4.cloned.1.call-update
  15.7 18.3 %all-reduce = f32[256]{0:T(256)S(1)} all-reduce(f32[256]{0:T(256)S(1)} %get-tuple-element.133), channel_id=2, replica_groups=mesh['dp'=4,'ctx'=8] {'ctx'}, use_global_device_ids=true, to_apply=%add | all-reduce | flops 256 | bytes 2048
  34.0 0.1 reshape.232
  34.1 0.1 compare_and_fusion
  34.2 0.1 subtract_maximum_fusion
  34.2 135.5 %all-gather.4.cloned.1.call-done = f32[256,128,128]{2,1,0:T(8,128)} async-done(((f32[32,128,128]{2,1,0:T(8,128)}), f32[256,128,128]{2,1,0:T(8,128)}) %all-gather.4.cloned.1.call-update) | async-done | bytes 16777232 | tf_op jit(solution)/shard_map/all_gather | solution.py:12
  169.7 17.1 %while.14 = (s32[]{:T(128)}, f32[32,128,128]{2,1,0:T(8,128)S(1)}, s32[]{:T(128)}, f32[8,32]{1,0:T(8,128)S(1)}, f32[8,32,128,128]{3,2,1,0:T(8,128)}, /*index=5*/s32[]{:T(128)}, s32[]{:T(128)}) while((s32[]{:T(128)}, f32[32,128,128]{2,1,0:T(8,128)S(1)}, s32[]{:T(128)}, f32[8,32]{1,0:T(8,128)S(1)}, f32[8,32,128,128]{3,2,1,0:T(8,128)}, ...), condition=%wide.region_2.3_spmd.clone, body=%wide.region_1.2_spmd.clone.sunk | while | flops 2097156 | bytes 6291945 | solution.py:24
  169.7 2.1 %fusion.44 = f32[32,128,128]{2,1,0:T(8,128)S(1)} fusion(f32[8,32,128,128]{3,2,1,0:T(8,128)} %get-tuple-element.187, s32[]{:T(128)} %get-tuple-element.176, f32[32,128,128]{2,1,0:T(8,128)S(1)} %get-tuple-element.177, f32[32]{0:T(128)S(1)} %dynamic-slice_bitcast_fusion.2, pred[]{:T(512)S(6)} %compare.3, pred[]{:T(512)S(6)} %lt.22), kind=kLoop, calls=%fused_computation.1.clone.1 | loop fusion | flops 2097152 | bytes 6291590 | tf_op jit(solution)/shard_map/while/body/eval_jaxpr/jit(_where)/select_n | solution.py:22
  171.9 2.1 %fusion.44 = f32[32,128,128]{2,1,0:T(8,128)S(1)} fusion(f32[8,32,128,128]{3,2,1,0:T(8,128)} %get-tuple-element.187, s32[]{:T(128)} %get-tuple-element.176, f32[32,128,128]{2,1,0:T(8,128)S(1)} %get-tuple-element.177, f32[32]{0:T(128)S(1)} %dynamic-slice_bitcast_fusion.2, pred[]{:T(512)S(6)} %compare.3, pred[]{:T(512)S(6)} %lt.22), kind=kLoop, calls=%fused_computation.1.clone.1 | loop fusion | flops 2097152 | bytes 6291590 | tf_op jit(solution)/shard_map/while/body/eval_jaxpr/jit(_where)/select_n | solution.py:22
  174.0 2.1 %fusion.44 = f32[32,128,128]{2,1,0:T(8,128)S(1)} fusion(f32[8,32,128,128]{3,2,1,0:T(8,128)} %get-tuple-element.187, s32[]{:T(128)} %get-tuple-element.176, f32[32,128,128]{2,1,0:T(8,128)S(1)} %get-tuple-element.177, f32[32]{0:T(128)S(1)} %dynamic-slice_bitcast_fusion.2, pred[]{:T(512)S(6)} %compare.3, pred[]{:T(512)S(6)} %lt.22), kind=kLoop, calls=%fused_computation.1.clone.1 | loop fusion | flops 2097152 | bytes 6291590 | tf_op jit(solution)/shard_map/while/body/eval_jaxpr/jit(_where)/select_n | solution.py:22
  176.2 2.1 %fusion.44 = f32[32,128,128]{2,1,0:T(8,128)S(1)} fusion(f32[8,32,128,128]{3,2,1,0:T(8,128)} %get-tuple-element.187, s32[]{:T(128)} %get-tuple-element.176, f32[32,128,128]{2,1,0:T(8,128)S(1)} %get-tuple-element.177, f32[32]{0:T(128)S(1)} %dynamic-slice_bitcast_fusion.2, pred[]{:T(512)S(6)} %compare.3, pred[]{:T(512)S(6)} %lt.22), kind=kLoop, calls=%fused_computation.1.clone.1 | loop fusion | flops 2097152 | bytes 6291590 | tf_op jit(solution)/shard_map/while/body/eval_jaxpr/jit(_where)/select_n | solution.py:22
  178.3 2.1 %fusion.44 = f32[32,128,128]{2,1,0:T(8,128)S(1)} fusion(f32[8,32,128,128]{3,2,1,0:T(8,128)} %get-tuple-element.187, s32[]{:T(128)} %get-tuple-element.176, f32[32,128,128]{2,1,0:T(8,128)S(1)} %get-tuple-element.177, f32[32]{0:T(128)S(1)} %dynamic-slice_bitcast_fusion.2, pred[]{:T(512)S(6)} %compare.3, pred[]{:T(512)S(6)} %lt.22), kind=kLoop, calls=%fused_computation.1.clone.1 | loop fusion | flops 2097152 | bytes 6291590 | tf_op jit(solution)/shard_map/while/body/eval_jaxpr/jit(_where)/select_n | solution.py:22
  180.4 2.1 %fusion.44 = f32[32,128,128]{2,1,0:T(8,128)S(1)} fusion(f32[8,32,128,128]{3,2,1,0:T(8,128)} %get-tuple-element.187, s32[]{:T(128)} %get-tuple-element.176, f32[32,128,128]{2,1,0:T(8,128)S(1)} %get-tuple-element.177, f32[32]{0:T(128)S(1)} %dynamic-slice_bitcast_fusion.2, pred[]{:T(512)S(6)} %compare.3, pred[]{:T(512)S(6)} %lt.22), kind=kLoop, calls=%fused_computation.1.clone.1 | loop fusion | flops 2097152 | bytes 6291590 | tf_op jit(solution)/shard_map/while/body/eval_jaxpr/jit(_where)/select_n | solution.py:22
  182.6 2.1 %fusion.44 = f32[32,128,128]{2,1,0:T(8,128)S(1)} fusion(f32[8,32,128,128]{3,2,1,0:T(8,128)} %get-tuple-element.187, s32[]{:T(128)} %get-tuple-element.176, f32[32,128,128]{2,1,0:T(8,128)S(1)} %get-tuple-element.177, f32[32]{0:T(128)S(1)} %dynamic-slice_bitcast_fusion.2, pred[]{:T(512)S(6)} %compare.3, pred[]{:T(512)S(6)} %lt.22), kind=kLoop, calls=%fused_computation.1.clone.1 | loop fusion | flops 2097152 | bytes 6291590 | tf_op jit(solution)/shard_map/while/body/eval_jaxpr/jit(_where)/select_n | solution.py:22
  184.7 2.1 %fusion.44 = f32[32,128,128]{2,1,0:T(8,128)S(1)} fusion(f32[8,32,128,128]{3,2,1,0:T(8,128)} %get-tuple-element.187, s32[]{:T(128)} %get-tuple-element.176, f32[32,128,128]{2,1,0:T(8,128)S(1)} %get-tuple-element.177, f32[32]{0:T(128)S(1)} %dynamic-slice_bitcast_fusion.2, pred[]{:T(512)S(6)} %compare.3, pred[]{:T(512)S(6)} %lt.22), kind=kLoop, calls=%fused_computation.1.clone.1 | loop fusion | flops 2097152 | bytes 6291590 | tf_op jit(solution)/shard_map/while/body/eval_jaxpr/jit(_where)/select_n | solution.py:22
  186.8 0.0 copy-done.1
  186.8 1.4 fusion.2
  188.2 2.2 %multiply_reduce_fusion = (f32[64,32]{0,1:T(8,128)S(1)}, f32[64,32,128]{2,0,1:T(8,128)S(1)}) fusion(f32[64,32,128]{2,0,1:T(8,128)} %fusion.2, f32[64,64]{1,0:T(8,128)S(1)} %subtract_maximum_fusion, f32[32]{0:T(128)S(1)} %get-tuple-element.132, pred[64,64]{1,0:T(8,128)(4,1)S(1)} %compare_and_fusion, bf16[64,4096]{1,0:T(8,128)(2,1)S(1)} %copy-done, ...), kind=kOutput, calls=%fused_computation.10 | convolution fusion | flops 68417536 | bytes 3698816 | tf_op jit(solution)/shard_map/hij,jhd->ihd/dot_general | solution.py:36
  190.4 0.0 copy-done.2
  190.4 1.1 copy_bitcast_fusion
  (15 shorter events, 0.1 us)
Async XLA Ops:
  6.5 5.6 %copy-start = (bf16[64,4096]{1,0:T(8,128)(2,1)S(1)}, bf16[64,4096]{1,0:T(8,128)(2,1)}, u32[]{:S(2)}) copy-start(bf16[64,4096]{1,0:T(8,128)(2,1)} %param.10) | copy-start | bytes 1572868
  6.5 163.2 %all-gather.4.cloned.1.call-start = ((), (), s32[]{:S(2)}) async-start(), calls=%async_computation | async-start | bytes 18874368 | tf_op jit(solution)/shard_map/all_gather | solution.py:12
  169.7 17.1 %copy-start.1 = (bf16[64,4096]{1,0:T(8,128)(2,1)S(1)}, bf16[64,4096]{1,0:T(8,128)(2,1)}, u32[]{:S(2)}) copy-start(bf16[64,4096]{1,0:T(8,128)(2,1)} %param.8) | copy-start | bytes 1572868
  188.2 2.2 %copy-start.2 = (f32[4096]{0:T(1024)S(1)}, f32[4096]{0:T(1024)}, u32[]{:S(2)}) copy-start(f32[4096]{0:T(1024)} %param.13) | copy-start | bytes 49156
Sparse Core Ops, SparseCore 0:
  15.8 153.8 all-gather.3
where the time goes:
time: 199 us; the launch traced here: 198 us
  waiting for transfers between devices  135 us (68%)
  other arithmetic  19.8 us (10%)
  blocking collectives  18.3 us (9%)
  between operations  14.8 us (7%)
  matrix products  7.09 us (4%)
  local copies, waits for them, and re-layouts  2.71 us (1%)
    all_gather x1, waiting for transfers between devices, prefix(): everything = jax.tree.map(lambda part: lax.all_gather(part, axis), value)  135 us
    unnamed x1, blocking collectives  18.3 us
    select_n x8, other arithmetic, step(): return jax.tree.map(lambda a, b: jnp.where(reached, a, b), new, before)  16.8 us
  transfers between devices with their start and end apart: 1, of which 1 were waited for; matrix products, arithmetic and copies ran while one was open for 0% of the time, Pallas kernels for 0%

commit v1 on v0

v1 whole, which is shorter than its diff:
```python
import functools

import jax
import jax.numpy as jnp
from jax import lax
from jax.experimental import pallas as pl
from jax.experimental.pallas import tpu as pltpu
from jax.sharding import PartitionSpec as P

HEADS = 32
HEAD = 128
HALF = HEADS // 2
LAG = 2
F32 = jnp.float32
BF16 = jnp.bfloat16
MESH = pl.DeviceIdType.MESH


def kernel(
    chips, exps, doc, gain, q_hbm, k_hbm, v_hbm, o_ref,
    q, k, v, own, give, got, up_out, up_in, pass_out, pass_in, low, raw, flag_out, flag_in,
    load_sem, give_send, give_recv, up_send, up_recv, pass_send, pass_recv, flag_send, flag_recv,
):
    rows = q.shape[0]
    me = lax.axis_index("ctx")
    core, chip = lax.rem(me, 2), lax.div(me, 2)
    partner, above, below = me + 1 - 2 * core, me + 2, me - 2
    mine, theirs = core * HALF, (1 - core) * HALF

    def load(i, src, dst, first):
        cols = pl.ds(pl.multiple_of(first * HEAD, HALF * HEAD), HALF * HEAD)
        return pltpu.make_async_copy(src.at[:, cols], dst.at[:, cols], load_sem.at[i])

    loads = [
        load(0, k_hbm, k, theirs), load(1, v_hbm, v, theirs), load(2, k_hbm, k, mine),
        load(3, v_hbm, v, mine), load(4, q_hbm, q, mine), load(5, q_hbm, q, theirs),
    ]
    for c in loads:
        c.start()

    barrier = pltpu.get_barrier_semaphore()
    pl.semaphore_signal(barrier, inc=1, device_id={"ctx": partner}, device_id_type=MESH)

    @pl.when(chip > 0)
    def _():
        pl.semaphore_signal(barrier, inc=1, device_id={"ctx": below}, device_id_type=MESH)

    starts = doc[...].astype(F32)
    sub = lax.broadcasted_iota(jnp.int32, (rows, rows), 0)
    lane = lax.broadcasted_iota(jnp.int32, (rows, rows), 1)
    wide = jnp.broadcast_to(starts, (rows, rows))
    count_col = jnp.sum(jnp.where(lane <= sub, wide, 0.0), axis=1, keepdims=True)
    start_col = jnp.sum(jnp.where(lane == sub, wide, 0.0), axis=1, keepdims=True)
    count_row = jnp.sum(jnp.where(sub <= lane, jnp.broadcast_to(start_col, (rows, rows)), 0.0), axis=0, keepdims=True)
    total = jnp.sum(starts, axis=1, keepdims=True)
    same = (count_col == count_row) & (sub >= lane)
    gaps = jnp.maximum(sub - lane, 0).astype(F32)
    place = lax.broadcasted_iota(jnp.int32, (rows, HEAD), 0).astype(F32)
    fresh = jnp.broadcast_to(jnp.where(count_col == 0.0, 1.0, 0.0), (rows, HEAD))
    trail = jnp.broadcast_to(jnp.where(count_col == total, 1.0, 0.0), (rows, HEAD))
    whole = jnp.where(total == 0.0, 1.0, 0.0)
    flag_out[...] = jnp.broadcast_to(whole, flag_out.shape)

    def columns(h):
        return pl.ds(pl.multiple_of(h * HEAD, HEAD), HEAD)

    def rate_of(h):
        return exps[h].astype(F32) * (1.0 / 65536.0)

    def state(h):
        scale = jnp.exp(-rate_of(h) * (rows - 1.0 - place)) * trail
        kd = (k[:, columns(h)].astype(F32) * scale).astype(BF16)
        return lax.dot_general(kd, v[:, columns(h)], (((0,), (0,)), ((), ())), preferred_element_type=F32)

    def remote(src, dst, ssem, rsem, dev):
        return pltpu.make_async_remote_copy(
            src_ref=src, dst_ref=dst, send_sem=ssem, recv_sem=rsem, device_id={"ctx": dev}, device_id_type=MESH
        )

    def give_copy(g):
        return remote(give.at[g], got.at[g], give_send.at[g], give_recv.at[g], partner)

    def up_copy(g):
        return remote(up_out.at[g], up_in.at[g], up_send.at[g], up_recv.at[g], above)

    def pass_copy(g):
        return remote(pass_out.at[g], pass_in.at[g], pass_send.at[g], pass_recv.at[g], partner)

    flag_copy = remote(flag_out, flag_in, flag_send.at[0], flag_recv.at[0], partner)

    def chain(g, first):
        give_copy(g).wait_recv()
        held, other = own[g], got[g].astype(F32)
        at0 = core == 0
        s0, s1 = jnp.where(at0, held, other), jnp.where(at0, other, held)
        full = jnp.exp(jnp.full((1, HEAD), -rate_of(mine + g) * rows, F32))
        f_me, f_partner = full * flag_out[0:1, :], full * flag_in[0:1, :]
        f0, f1 = jnp.where(at0, f_me, f_partner), jnp.where(at0, f_partner, f_me)
        if first:
            before = jnp.zeros((HEAD, HEAD), F32)
            middle = s0
        else:
            up_copy(g).wait_recv()
            before = up_in[g].astype(F32)
            middle = f0 * before + s0

        @pl.when(chip < chips - 1)
        def _():
            up_out[g] = (f1 * middle + s1).astype(BF16)
            up_copy(g).start()

        pass_out[g] = jnp.where(at0, middle, before).astype(BF16)
        pass_copy(g).start()
        low[g] = jnp.where(at0, before, middle).astype(BF16)

    def intra(h):
        cols = columns(h)
        scores = lax.dot_general(q[:, cols], k[:, cols], (((1,), (1,)), ((), ())), preferred_element_type=F32)
        weight = jnp.where(same, jnp.exp(-rate_of(h) * gaps), 0.0)
        raw[:, cols] = jnp.dot((scores * weight).astype(BF16), v[:, cols], preferred_element_type=F32)

    def output(h, carry):
        cols = columns(h)
        qscale = jnp.exp(-rate_of(h) * (place + 1.0)) * fresh
        r = raw[:, cols] + qscale * jnp.dot(q[:, cols], carry, preferred_element_type=F32)
        meansq = jnp.mean(r * r, axis=-1, keepdims=True)
        o_ref[:, cols] = (r * lax.rsqrt(meansq + 1e-06) * gain[pl.ds(h, 1), :]).astype(BF16)

    loads[0].wait()
    loads[1].wait()
    pl.semaphore_wait(barrier, jnp.where(chip < chips - 1, 2, 1))
    flag_copy.start()
    loads[2].wait()
    loads[3].wait()

    def step_a(g, _):
        @pl.when(g < HALF)
        def _():
            give[g] = state(theirs + g).astype(BF16)
            give_copy(g).start()
            own[g] = state(mine + g)

        @pl.when(g == LAG)
        def _():
            flag_copy.wait_recv()

        @pl.when((g >= LAG) & (chip == 0))
        def _():
            chain(g - LAG, True)

        return 0

    lax.fori_loop(0, HALF + LAG, step_a, 0)
    loads[4].wait()
    loads[5].wait()

    def both(g):
        intra(mine + g)
        intra(theirs + g)

    @pl.when(chip >= 2)
    def _():
        lax.fori_loop(0, HALF, lambda g, _: (both(g), 0)[1], 0)

    def step_c(g, _):
        @pl.when((g < HALF) & (chip > 0))
        def _():
            chain(g, False)

        @pl.when((g < HALF) & (chip < 2))
        def _():
            both(g)

        @pl.when(g >= LAG)
        def _():
            e = g - LAG
            output(mine + e, low[e])
            pass_copy(e).wait_recv()
            output(theirs + e, pass_in[e])

        return 0

    lax.fori_loop(0, HALF + LAG, step_c, 0)

    flag_copy.wait_send()

    def drain(g, _):
        give_copy(g).wait_send()
        pass_copy(g).wait_send()

        @pl.when(chip < chips - 1)
        def _():
            up_copy(g).wait_send()

        return 0

    lax.fori_loop(0, HALF, drain, 0)


def on_device(queries, keys, values, doc_starts, decay_exps, norm_gain):
    rows = queries.shape[0]
    chips = lax.axis_size("ctx") // 2
    vmem, smem, anywhere = (pl.BlockSpec(memory_space=m) for m in (pltpu.VMEM, pltpu.SMEM, pl.ANY))
    half = (HALF, HEAD, HEAD)
    sem = pltpu.SemaphoreType.DMA
    return pl.pallas_call(
        functools.partial(kernel, chips),
        out_shape=jax.ShapeDtypeStruct(queries.shape, BF16),
        in_specs=[smem, vmem, vmem, anywhere, anywhere, anywhere],
        out_specs=vmem,
        scratch_shapes=[
            *[pltpu.VMEM(queries.shape, BF16)] * 3,
            pltpu.VMEM(half, F32),
            *[pltpu.VMEM(half, BF16)] * 7,
            pltpu.VMEM(queries.shape, F32),
            pltpu.VMEM((8, HEAD), F32),
            pltpu.VMEM((8, HEAD), F32),
            sem((6,)),
            *[sem((HALF,))] * 6,
            sem((1,)),
            sem((1,)),
        ],
        compiler_params=pltpu.CompilerParams(
            collective_id=0, has_side_effects=True, vmem_limit_bytes=32 * 2**20
        ),
        name="chain",
    )(
        decay_exps,
        doc_starts.reshape(1, rows),
        norm_gain.reshape(HEADS, HEAD),
        queries, keys, values,
    )


def solution(mesh):
    return jax.shard_map(
        on_device,
        mesh=mesh,
        in_specs=(
            P(("dp", "ctx"), None),
            P(("dp", "ctx"), None),
            P(("dp", "ctx"), None),
            P(("dp", "ctx")),
            P(),
            P(),
        ),
        out_specs=P(("dp", "ctx"), None),
        check_vma=False,
    )
```

time: 199 us -> 36.1 us (0.18)
  the two profiles are of different devices: /device:TPU:0 before, /device:TPU:31 now
where the time goes in v1:
time: 36.1 us; the launch traced here: 35.8 us
  Pallas kernels  30.5 us (84%)
  local copies, waits for them, and re-layouts  5.31 us (15%)
    pallas_call x1, Pallas kernels, on_device(): pl.pallas_call(functools.partial(kernel, chips), out_shape=jax.ShapeDtype...  30.5 us
    unnamed x13, local copies, waits for them, and re-layouts  5.31 us

profile of v1, /device:TPU:31, one launch (start us, length us, event | category | flops | bytes accessed | tf_op | source)
XLA Modules:
  0.0 35.8 jit_solution(8127425237578750695)
XLA Ops:
  0.0 0.0 copy-start.4
  0.0 0.0 copy-start.5
  0.0 0.7 %copy-done.4 = s32[32]{0:T(128)S(1)} copy-done((s32[32]{0:T(128)S(1)}, s32[32]{0:T(128)}, u32[]{:S(2)}) %copy-start.4) | copy-done | bytes 152
  0.7 0.0 copy-done.5
  0.7 0.0 copy-start
  0.7 1.0 %copy-done = bf16[64,4096]{1,0:T(8,128)(2,1)S(1)} copy-done((bf16[64,4096]{1,0:T(8,128)(2,1)S(1)}, bf16[64,4096]{1,0:T(8,128)(2,1)}, u32[]{:S(2)}) %copy-start) | copy-done | bytes 524312
  1.7 0.0 copy-start.1
  1.7 1.0 %copy-done.1 = bf16[64,4096]{1,0:T(8,128)(2,1)S(1)} copy-done((bf16[64,4096]{1,0:T(8,128)(2,1)S(1)}, bf16[64,4096]{1,0:T(8,128)(2,1)}, u32[]{:S(2)}) %copy-start.1) | copy-done | bytes 524312
  2.8 0.0 copy-start.2
  2.8 1.0 %copy-done.2 = bf16[64,4096]{1,0:T(8,128)(2,1)S(1)} copy-done((bf16[64,4096]{1,0:T(8,128)(2,1)S(1)}, bf16[64,4096]{1,0:T(8,128)(2,1)}, u32[]{:S(2)}) %copy-start.2) | copy-done | bytes 524312
  3.8 0.0 copy-start.3
  3.8 0.7 %copy-done.3 = f32[4096]{0:T(1024)S(1)} copy-done((f32[4096]{0:T(1024)S(1)}, f32[4096]{0:T(1024)}, u32[]{:S(2)}) %copy-start.3) | copy-done | bytes 16408
  4.5 30.5 %chain.1 = bf16[64,4096]{1,0:T(8,128)(2,1)S(1)} custom-call(s32[32]{0:T(128)S(1)} %copy-done.4, s32[1,64]{1,0:T(1,128)S(1)} %bitcast.3, f32[32,128]{1,0:T(8,128)S(1)} %bitcast.2, bf16[64,4096]{1,0:T(8,128)(2,1)S(1)} %copy-done, bf16[64,4096]{1,0:T(8,128)(2,1)S(1)} %copy-done.1, bf16[64,4096]{1,0:T(8,128)(2,1)S(1)} %copy-done.2), custom_call_target="tpu_custom_call" | custom-call | tf_op jit(solution)/shard_map/chain/pallas_call | solution.py:206
  35.0 0.8 %copy.8 = bf16[64,4096]{1,0:T(8,128)(2,1)} copy(bf16[64,4096]{1,0:T(8,128)(2,1)S(1)} %chain.1) | data formatting | bytes 1048576
Async XLA Ops:
  0.0 0.7 %copy-start.4 = (s32[32]{0:T(128)S(1)}, s32[32]{0:T(128)}, u32[]{:S(2)}) copy-start(s32[32]{0:T(128)} %exps.1) | copy-start | bytes 388
  0.0 0.7 %copy-start.5 = (s32[64]{0:T(128)S(1)}, s32[64]{0:T(128)}, u32[]{:S(2)}) copy-start(s32[64]{0:T(128)} %param.9) | copy-start | bytes 772
  0.7 1.0 %copy-start = (bf16[64,4096]{1,0:T(8,128)(2,1)S(1)}, bf16[64,4096]{1,0:T(8,128)(2,1)}, u32[]{:S(2)}) copy-start(bf16[64,4096]{1,0:T(8,128)(2,1)} %q_hbm.1) | copy-start | bytes 1572868
  1.7 1.0 %copy-start.1 = (bf16[64,4096]{1,0:T(8,128)(2,1)S(1)}, bf16[64,4096]{1,0:T(8,128)(2,1)}, u32[]{:S(2)}) copy-start(bf16[64,4096]{1,0:T(8,128)(2,1)} %k_hbm.1) | copy-start | bytes 1572868
  2.8 1.0 %copy-start.2 = (bf16[64,4096]{1,0:T(8,128)(2,1)S(1)}, bf16[64,4096]{1,0:T(8,128)(2,1)}, u32[]{:S(2)}) copy-start(bf16[64,4096]{1,0:T(8,128)(2,1)} %v_hbm.1) | copy-start | bytes 1572868
  3.8 0.7 %copy-start.3 = (f32[4096]{0:T(1024)S(1)}, f32[4096]{0:T(1024)}, u32[]{:S(2)}) copy-start(f32[4096]{0:T(1024)} %param.11) | copy-start | bytes 49156

commit v2 on v1

--- a/solution.py
+++ b/solution.py
@@ -10,15 +10,16 @@
 HEADS = 32
 HEAD = 128
 HALF = HEADS // 2
-LAG = 2
+UNROLL = 2
+STEPS = HALF // UNROLL
 F32 = jnp.float32
 BF16 = jnp.bfloat16
 MESH = pl.DeviceIdType.MESH
 
 
 def kernel(
-    chips, exps, doc, gain, q_hbm, k_hbm, v_hbm, o_ref,
-    q, k, v, own, give, got, up_out, up_in, pass_out, pass_in, low, raw, flag_out, flag_in,
+    chips, exps_hbm, doc_hbm, gain_hbm, q_hbm, k_hbm, v_hbm, o_ref,
+    exps, doc, gain, q, k, v, own, give, got, up_out, up_in, pass_out, pass_in, low, raw, flag_out, flag_in,
     load_sem, give_send, give_recv, up_send, up_recv, pass_send, pass_recv, flag_send, flag_recv,
 ):
     rows = q.shape[0]
@@ -35,7 +36,11 @@
         load(0, k_hbm, k, theirs), load(1, v_hbm, v, theirs), load(2, k_hbm, k, mine),
         load(3, v_hbm, v, mine), load(4, q_hbm, q, mine), load(5, q_hbm, q, theirs),
     ]
-    for c in loads:
+    small = [
+        pltpu.make_async_copy(src, dst, load_sem.at[6 + i])
+        for i, (src, dst) in enumerate(((doc_hbm, doc), (exps_hbm, exps), (gain_hbm, gain)))
+    ]
+    for c in small + loads:
         c.start()
 
     barrier = pltpu.get_barrier_semaphore()
@@ -45,6 +50,8 @@
     def _():
         pl.semaphore_signal(barrier, inc=1, device_id={"ctx": below}, device_id_type=MESH)
 
+    for c in small:
+        c.wait()
     starts = doc[...].astype(F32)
     sub = lax.broadcasted_iota(jnp.int32, (rows, rows), 0)
     lane = lax.broadcasted_iota(jnp.int32, (rows, rows), 1)
@@ -88,43 +95,71 @@
 
     flag_copy = remote(flag_out, flag_in, flag_send.at[0], flag_recv.at[0], partner)
 
-    def chain(g, first):
-        give_copy(g).wait_recv()
-        held, other = own[g], got[g].astype(F32)
+    def chain(step, first):
         at0 = core == 0
-        s0, s1 = jnp.where(at0, held, other), jnp.where(at0, other, held)
-        full = jnp.exp(jnp.full((1, HEAD), -rate_of(mine + g) * rows, F32))
-        f_me, f_partner = full * flag_out[0:1, :], full * flag_in[0:1, :]
-        f0, f1 = jnp.where(at0, f_me, f_partner), jnp.where(at0, f_partner, f_me)
-        if first:
-            before = jnp.zeros((HEAD, HEAD), F32)
-            middle = s0
-        else:
-            up_copy(g).wait_recv()
-            before = up_in[g].astype(F32)
-            middle = f0 * before + s0
+        heads = [step * UNROLL + u for u in range(UNROLL)]
+        for g in heads:
+            give_copy(g).wait_recv()
+            if not first:
+                up_copy(g).wait_recv()
+        ups, passes, lows = [], [], []
+        for g in heads:
+            held, other = own[g], got[g].astype(F32)
+            s0, s1 = jnp.where(at0, held, other), jnp.where(at0, other, held)
+            full = jnp.exp(jnp.full((1, HEAD), -rate_of(mine + g) * rows, F32))
+            f_me, f_partner = full * flag_out[0:1, :], full * flag_in[0:1, :]
+            f0, f1 = jnp.where(at0, f_me, f_partner), jnp.where(at0, f_partner, f_me)
+            if first:
+                before = jnp.zeros((HEAD, HEAD), F32)
+                middle = s0
+            else:
+                before = up_in[g].astype(F32)
+                middle = f0 * before + s0
+            ups.append((f1 * middle + s1).astype(BF16))
+            passes.append(jnp.where(at0, middle, before).astype(BF16))
+            lows.append(jnp.where(at0, before, middle).astype(BF16))
+        for g, a, b, c in zip(heads, ups, passes, lows):
+            up_out[g], pass_out[g], low[g] = a, b, c
 
         @pl.when(chip < chips - 1)
         def _():
-            up_out[g] = (f1 * middle + s1).astype(BF16)
-            up_copy(g).start()
-
-        pass_out[g] = jnp.where(at0, middle, before).astype(BF16)
-        pass_copy(g).start()
-        low[g] = jnp.where(at0, before, middle).astype(BF16)
-
-    def intra(h):
-        cols = columns(h)
-        scores = lax.dot_general(q[:, cols], k[:, cols], (((1,), (1,)), ((), ())), preferred_element_type=F32)
-        weight = jnp.where(same, jnp.exp(-rate_of(h) * gaps), 0.0)
-        raw[:, cols] = jnp.dot((scores * weight).astype(BF16), v[:, cols], preferred_element_type=F32)
-
-    def output(h, carry):
-        cols = columns(h)
-        qscale = jnp.exp(-rate_of(h) * (place + 1.0)) * fresh
-        r = raw[:, cols] + qscale * jnp.dot(q[:, cols], carry, preferred_element_type=F32)
-        meansq = jnp.mean(r * r, axis=-1, keepdims=True)
-        o_ref[:, cols] = (r * lax.rsqrt(meansq + 1e-06) * gain[pl.ds(h, 1), :]).astype(BF16)
+            for g in heads:
+                up_copy(g).start()
+
+        for g in heads:
+            pass_copy(g).start()
+
+    def pairs(step):
+        return [step * UNROLL + u for u in range(UNROLL)]
+
+    def both(step):
+        heads = [first + g for first in (mine, theirs) for g in pairs(step)]
+        scores = [
+            lax.dot_general(q[:, columns(h)], k[:, columns(h)], (((1,), (1,)), ((), ())), preferred_element_type=F32)
+            for h in heads
+        ]
+        weighted = [
+            (x * jnp.where(same, jnp.exp(-rate_of(h) * gaps), 0.0)).astype(BF16) for x, h in zip(scores, heads)
+        ]
+        sums = [jnp.dot(w, v[:, columns(h)], preferred_element_type=F32) for w, h in zip(weighted, heads)]
+        for x, h in zip(sums, heads):
+            raw[:, columns(h)] = x
+
+    def output(step):
+        for g in pairs(step):
+            pass_copy(g).wait_recv()
+        heads = [first + g for first in (mine, theirs) for g in pairs(step)]
+        carries = [ref[g] for ref in (low, pass_in) for g in pairs(step)]
+        cross = [jnp.dot(q[:, columns(h)], c, preferred_element_type=F32) for h, c in zip(heads, carries)]
+        raws = [
+            raw[:, columns(h)] + jnp.exp(-rate_of(h) * (place + 1.0)) * fresh * x for h, x in zip(heads, cross)
+        ]
+        means = [jnp.mean(r * r, axis=-1, keepdims=True) for r in raws]
+        outs = [
+            (r * lax.rsqrt(m + 1e-06) * gain[pl.ds(h, 1), :]).astype(BF16) for r, m, h in zip(raws, means, heads)
+        ]
+        for x, h in zip(outs, heads):
+            o_ref[:, columns(h)] = x
 
     loads[0].wait()
     loads[1].wait()
@@ -133,54 +168,50 @@
     loads[2].wait()
     loads[3].wait()
 
-    def step_a(g, _):
-        @pl.when(g < HALF)
-        def _():
-            give[g] = state(theirs + g).astype(BF16)
-            give_copy(g).start()
-            own[g] = state(mine + g)
-
-        @pl.when(g == LAG)
+    def step_a(step, _):
+        @pl.when(step < STEPS)
+        def _():
+            give_now = [state(theirs + g).astype(BF16) for g in pairs(step)]
+            own_now = [state(mine + g) for g in pairs(step)]
+            for g, a, b in zip(pairs(step), give_now, own_now):
+                give[g], own[g] = a, b
+            for g in pairs(step):
+                give_copy(g).start()
+
+        @pl.when(step == 1)
         def _():
             flag_copy.wait_recv()
 
-        @pl.when((g >= LAG) & (chip == 0))
-        def _():
-            chain(g - LAG, True)
+        @pl.when((step >= 1) & (chip == 0))
+        def _():
+            chain(step - 1, True)
 
         return 0
 
-    lax.fori_loop(0, HALF + LAG, step_a, 0)
+    lax.fori_loop(0, STEPS + 1, step_a, 0)
     loads[4].wait()
     loads[5].wait()
 
-    def both(g):
-        intra(mine + g)
-        intra(theirs + g)
-
     @pl.when(chip >= 2)
     def _():
-        lax.fori_loop(0, HALF, lambda g, _: (both(g), 0)[1], 0)
-
-    def step_c(g, _):
-        @pl.when((g < HALF) & (chip > 0))
-        def _():
-            chain(g, False)
-
-        @pl.when((g < HALF) & (chip < 2))
-        def _():
-            both(g)
-
-        @pl.when(g >= LAG)
-        def _():
-            e = g - LAG
-            output(mine + e, low[e])
-            pass_copy(e).wait_recv()
-            output(theirs + e, pass_in[e])
+        lax.fori_loop(0, STEPS, lambda step, _: (both(step), 0)[1], 0)
+
+    def step_c(step, _):
+        @pl.when((step < STEPS) & (chip > 0))
+        def _():
+            chain(step, False)
+
+        @pl.when((step < STEPS) & (chip < 2))
+        def _():
+            both(step)
+
+        @pl.when(step >= 1)
+        def _():
+            output(step - 1)
 
         return 0
 
-    lax.fori_loop(0, HALF + LAG, step_c, 0)
+    lax.fori_loop(0, STEPS + 1, step_c, 0)
 
     flag_copy.wait_send()
 
@@ -200,28 +231,31 @@
 def on_device(queries, keys, values, doc_starts, decay_exps, norm_gain):
     rows = queries.shape[0]
     chips = lax.axis_size("ctx") // 2
-    vmem, smem, anywhere = (pl.BlockSpec(memory_space=m) for m in (pltpu.VMEM, pltpu.SMEM, pl.ANY))
+    vmem, hbm = (pl.BlockSpec(memory_space=m) for m in (pltpu.VMEM, pltpu.HBM))
     half = (HALF, HEAD, HEAD)
     sem = pltpu.SemaphoreType.DMA
     return pl.pallas_call(
         functools.partial(kernel, chips),
         out_shape=jax.ShapeDtypeStruct(queries.shape, BF16),
-        in_specs=[smem, vmem, vmem, anywhere, anywhere, anywhere],
+        in_specs=[hbm] * 6,
         out_specs=vmem,
         scratch_shapes=[
+            pltpu.SMEM((HEADS,), jnp.int32),
+            pltpu.VMEM((1, rows), jnp.int32),
+            pltpu.VMEM((HEADS, HEAD), F32),
             *[pltpu.VMEM(queries.shape, BF16)] * 3,
             pltpu.VMEM(half, F32),
             *[pltpu.VMEM(half, BF16)] * 7,
             pltpu.VMEM(queries.shape, F32),
             pltpu.VMEM((8, HEAD), F32),
             pltpu.VMEM((8, HEAD), F32),
-            sem((6,)),
+            sem((9,)),
             *[sem((HALF,))] * 6,
             sem((1,)),
             sem((1,)),
         ],
         compiler_params=pltpu.CompilerParams(
-            collective_id=0, has_side_effects=True, vmem_limit_bytes=32 * 2**20
+            collective_id=0, has_side_effects=True, vmem_limit_bytes=60 * 2**20
         ),
         name="chain",
     )(

time: 36.1 us -> 27.1 us (0.75)
  Pallas kernels: 30.5 us -> 25 us
  local copies, waits for them, and re-layouts: 5.31 us -> 1.87 us
    pallas_call x1, Pallas kernels: 30.5 us -> 25 us  [on_device(): pl.pallas_call(functools.partial(kernel, chips), out_shape=jax.ShapeDtype...]
    unnamed x13 -> x1, local copies, waits for them, and re-layouts: 5.31 us -> 1.87 us
where the time goes in v2:
time: 27.1 us; the launch traced here: 26.9 us
  Pallas kernels  25 us (92%)
  local copies, waits for them, and re-layouts  1.87 us (7%)
    pallas_call x1, Pallas kernels, on_device(): pl.pallas_call(functools.partial(kernel, chips), out_shape=jax.ShapeDtype...  25 us
    unnamed x1, local copies, waits for them, and re-layouts  1.87 us

profile of v2, /device:TPU:31, one launch (start us, length us, event | category | flops | bytes accessed | tf_op | source)
XLA Modules:
  0.0 26.9 jit_solution(3359529089794216451)
XLA Ops:
  0.0 25.0 %chain.1 = bf16[64,4096]{1,0:T(8,128)(2,1)} custom-call(s32[32]{0:T(128)} %exps_hbm.1, s32[1,64]{1,0:T(1,128)} %bitcast.3, f32[32,128]{1,0:T(8,128)} %bitcast.2, bf16[64,4096]{1,0:T(8,128)(2,1)} %q_hbm.1, bf16[64,4096]{1,0:T(8,128)(2,1)} %k_hbm.1, bf16[64,4096]{1,0:T(8,128)(2,1)} %v_hbm.1), custom_call_target="tpu_custom_call" | custom-call | tf_op jit(solution)/shard_map/chain/pallas_call | solution.py:237
  25.0 1.9 %copy.8 = bf16[64,4096]{1,0:T(8,128)(2,1)} copy(bf16[64,4096]{1,0:T(8,128)(2,1)} %chain.1) | data formatting | bytes 1048576

commit v3 on v2

--- a/solution.py
+++ b/solution.py
@@ -12,6 +12,8 @@
 HALF = HEADS // 2
 UNROLL = 2
 STEPS = HALF // UNROLL
+PIECES = 2
+PIECE = HEAD // PIECES
 F32 = jnp.float32
 BF16 = jnp.bfloat16
 MESH = pl.DeviceIdType.MESH
@@ -87,8 +89,10 @@
     def give_copy(g):
         return remote(give.at[g], got.at[g], give_send.at[g], give_recv.at[g], partner)
 
-    def up_copy(g):
-        return remote(up_out.at[g], up_in.at[g], up_send.at[g], up_recv.at[g], above)
+    def up_copy(g, p):
+        part = (g, pl.ds(p * PIECE, PIECE))
+        i = g * PIECES + p
+        return remote(up_out.at[part], up_in.at[part], up_send.at[i], up_recv.at[i], above)
 
     def pass_copy(g):
         return remote(pass_out.at[g], pass_in.at[g], pass_send.at[g], pass_recv.at[g], partner)
@@ -97,36 +101,31 @@
 
     def chain(step, first):
         at0 = core == 0
-        heads = [step * UNROLL + u for u in range(UNROLL)]
-        for g in heads:
+        for u in range(UNROLL):
+            g = step * UNROLL + u
             give_copy(g).wait_recv()
-            if not first:
-                up_copy(g).wait_recv()
-        ups, passes, lows = [], [], []
-        for g in heads:
-            held, other = own[g], got[g].astype(F32)
-            s0, s1 = jnp.where(at0, held, other), jnp.where(at0, other, held)
             full = jnp.exp(jnp.full((1, HEAD), -rate_of(mine + g) * rows, F32))
             f_me, f_partner = full * flag_out[0:1, :], full * flag_in[0:1, :]
             f0, f1 = jnp.where(at0, f_me, f_partner), jnp.where(at0, f_partner, f_me)
-            if first:
-                before = jnp.zeros((HEAD, HEAD), F32)
-                middle = s0
-            else:
-                before = up_in[g].astype(F32)
-                middle = f0 * before + s0
-            ups.append((f1 * middle + s1).astype(BF16))
-            passes.append(jnp.where(at0, middle, before).astype(BF16))
-            lows.append(jnp.where(at0, before, middle).astype(BF16))
-        for g, a, b, c in zip(heads, ups, passes, lows):
-            up_out[g], pass_out[g], low[g] = a, b, c
-
-        @pl.when(chip < chips - 1)
-        def _():
-            for g in heads:
-                up_copy(g).start()
-
-        for g in heads:
+            for p in range(PIECES):
+                part = (g, pl.ds(p * PIECE, PIECE))
+                held, other = own[part], got[part].astype(F32)
+                s0, s1 = jnp.where(at0, held, other), jnp.where(at0, other, held)
+                if first:
+                    before = jnp.zeros((PIECE, HEAD), F32)
+                    middle = s0
+                else:
+                    up_copy(g, p).wait_recv()
+                    before = up_in[part].astype(F32)
+                    middle = f0 * before + s0
+                up_out[part] = (f1 * middle + s1).astype(BF16)
+
+                @pl.when(chip < chips - 1)
+                def _():
+                    up_copy(g, p).start()
+
+                pass_out[part] = jnp.where(at0, middle, before).astype(BF16)
+                low[part] = jnp.where(at0, before, middle).astype(BF16)
             pass_copy(g).start()
 
     def pairs(step):
@@ -146,20 +145,22 @@
             raw[:, columns(h)] = x
 
     def output(step):
-        for g in pairs(step):
-            pass_copy(g).wait_recv()
-        heads = [first + g for first in (mine, theirs) for g in pairs(step)]
-        carries = [ref[g] for ref in (low, pass_in) for g in pairs(step)]
-        cross = [jnp.dot(q[:, columns(h)], c, preferred_element_type=F32) for h, c in zip(heads, carries)]
-        raws = [
-            raw[:, columns(h)] + jnp.exp(-rate_of(h) * (place + 1.0)) * fresh * x for h, x in zip(heads, cross)
-        ]
-        means = [jnp.mean(r * r, axis=-1, keepdims=True) for r in raws]
-        outs = [
-            (r * lax.rsqrt(m + 1e-06) * gain[pl.ds(h, 1), :]).astype(BF16) for r, m, h in zip(raws, means, heads)
-        ]
-        for x, h in zip(outs, heads):
-            o_ref[:, columns(h)] = x
+        for first, ref in ((mine, low), (theirs, pass_in)):
+            heads = [first + g for g in pairs(step)]
+            if ref is pass_in:
+                for g in pairs(step):
+                    pass_copy(g).wait_recv()
+            carries = [ref[g] for g in pairs(step)]
+            cross = [jnp.dot(q[:, columns(h)], c, preferred_element_type=F32) for h, c in zip(heads, carries)]
+            raws = [
+                raw[:, columns(h)] + jnp.exp(-rate_of(h) * (place + 1.0)) * fresh * x for h, x in zip(heads, cross)
+            ]
+            means = [jnp.mean(r * r, axis=-1, keepdims=True) for r in raws]
+            outs = [
+                (r * lax.rsqrt(m + 1e-06) * gain[pl.ds(h, 1), :]).astype(BF16) for r, m, h in zip(raws, means, heads)
+            ]
+            for x, h in zip(outs, heads):
+                o_ref[:, columns(h)] = x
 
     loads[0].wait()
     loads[1].wait()
@@ -172,11 +173,13 @@
         @pl.when(step < STEPS)
         def _():
             give_now = [state(theirs + g).astype(BF16) for g in pairs(step)]
-            own_now = [state(mine + g) for g in pairs(step)]
-            for g, a, b in zip(pairs(step), give_now, own_now):
-                give[g], own[g] = a, b
+            for g, a in zip(pairs(step), give_now):
+                give[g] = a
             for g in pairs(step):
                 give_copy(g).start()
+            own_now = [state(mine + g) for g in pairs(step)]
+            for g, b in zip(pairs(step), own_now):
+                own[g] = b
 
         @pl.when(step == 1)
         def _():
@@ -221,7 +224,8 @@
 
         @pl.when(chip < chips - 1)
         def _():
-            up_copy(g).wait_send()
+            for p in range(PIECES):
+                up_copy(g, p).wait_send()
 
         return 0
 
@@ -250,19 +254,26 @@
             pltpu.VMEM((8, HEAD), F32),
             pltpu.VMEM((8, HEAD), F32),
             sem((9,)),
-            *[sem((HALF,))] * 6,
+            *[sem((HALF,))] * 2,
+            *[sem((HALF * PIECES,))] * 2,
+            *[sem((HALF,))] * 2,
             sem((1,)),
             sem((1,)),
         ],
         compiler_params=pltpu.CompilerParams(
-            collective_id=0, has_side_effects=True, vmem_limit_bytes=60 * 2**20
+            collective_id=0, has_side_effects=True, vmem_limit_bytes=32 * 2**20
         ),
         name="chain",
     )(
-        decay_exps,
-        doc_starts.reshape(1, rows),
-        norm_gain.reshape(HEADS, HEAD),
-        queries, keys, values,
+        *[
+            pltpu.with_memory_space_constraint(a, pltpu.HBM)
+            for a in (
+                decay_exps,
+                doc_starts.reshape(1, rows),
+                norm_gain.reshape(HEADS, HEAD),
+                queries, keys, values,
+            )
+        ]
     )
 
 

time: 27.1 us -> 24.2 us (0.89)
  Pallas kernels: 25 us -> 23.3 us
  local copies, waits for them, and re-layouts: 1.87 us -> 0.8 us
    pallas_call x1, Pallas kernels: 25 us -> 23.3 us  [on_device(): pl.pallas_call(functools.partial(kernel, chips), out_shape=jax.ShapeDtype...]
    unnamed x1, local copies, waits for them, and re-layouts: 1.87 us -> 0.8 us
where the time goes in v3:
time: 24.2 us; the launch traced here: 24.1 us
  Pallas kernels  23.3 us (96%)
  local copies, waits for them, and re-layouts  0.8 us (3%)
    pallas_call x1, Pallas kernels, on_device(): pl.pallas_call(functools.partial(kernel, chips), out_shape=jax.ShapeDtype...  23.3 us
    unnamed x1, local copies, waits for them, and re-layouts  0.8 us

profile of v3, /device:TPU:31, one launch (start us, length us, event | category | flops | bytes accessed | tf_op | source)
XLA Modules:
  0.0 24.1 jit_solution(902634578456808120)
XLA Ops:
  0.0 23.3 %chain.1 = bf16[64,4096]{1,0:T(8,128)(2,1)S(1)} custom-call(s32[32]{0:T(128)} %exps_hbm.1, s32[1,64]{1,0:T(1,128)} %bitcast.3, f32[32,128]{1,0:T(8,128)} %bitcast.2, bf16[64,4096]{1,0:T(8,128)(2,1)} %q_hbm.1, bf16[64,4096]{1,0:T(8,128)(2,1)} %k_hbm.1, bf16[64,4096]{1,0:T(8,128)(2,1)} %v_hbm.1), custom_call_target="tpu_custom_call" | custom-call | tf_op jit(solution)/shard_map/chain/pallas_call | solution.py:241
  23.3 0.8 %copy.8 = bf16[64,4096]{1,0:T(8,128)(2,1)} copy(bf16[64,4096]{1,0:T(8,128)(2,1)S(1)} %chain.1) | data formatting | bytes 1048576

commit v4 on v3

--- a/solution.py
+++ b/solution.py
@@ -208,13 +208,17 @@
         def _():
             both(step)
 
-        @pl.when(step >= 1)
+        @pl.when((step >= 1) & (chip != 1))
         def _():
             output(step - 1)
 
         return 0
 
     lax.fori_loop(0, STEPS + 1, step_c, 0)
+
+    @pl.when(chip == 1)
+    def _():
+        lax.fori_loop(0, STEPS, lambda step, _: (output(step), 0)[1], 0)
 
     flag_copy.wait_send()
 

time: 24.2 us -> 24.2 us (level)
  no operation moved by 1% of the time
where the time goes in v4:
time: 24.2 us; the launch traced here: 24.1 us
  Pallas kernels  23.3 us (96%)
  local copies, waits for them, and re-layouts  0.8 us (3%)
    pallas_call x1, Pallas kernels, on_device(): pl.pallas_call(functools.partial(kernel, chips), out_shape=jax.ShapeDtype...  23.3 us
    unnamed x1, local copies, waits for them, and re-layouts  0.8 us

profile of v4, /device:TPU:31, one launch (start us, length us, event | category | flops | bytes accessed | tf_op | source)
XLA Modules:
  0.0 24.1 jit_solution(9192762833404395320)
XLA Ops:
  0.0 23.3 %chain.1 = bf16[64,4096]{1,0:T(8,128)(2,1)S(1)} custom-call(s32[32]{0:T(128)} %exps_hbm.1, s32[1,64]{1,0:T(1,128)} %bitcast.3, f32[32,128]{1,0:T(8,128)} %bitcast.2, bf16[64,4096]{1,0:T(8,128)(2,1)} %q_hbm.1, bf16[64,4096]{1,0:T(8,128)(2,1)} %k_hbm.1, bf16[64,4096]{1,0:T(8,128)(2,1)} %v_hbm.1), custom_call_target="tpu_custom_call" | custom-call | tf_op jit(solution)/shard_map/chain/pallas_call | solution.py:245
  23.3 0.8 %copy.8 = bf16[64,4096]{1,0:T(8,128)(2,1)} copy(bf16[64,4096]{1,0:T(8,128)(2,1)S(1)} %chain.1) | data formatting | bytes 1048576

commit v5 on v4

--- a/solution.py
+++ b/solution.py
@@ -99,9 +99,9 @@
 
     flag_copy = remote(flag_out, flag_in, flag_send.at[0], flag_recv.at[0], partner)
 
-    def chain(step, first):
+    def chain(step, first, us=range(UNROLL)):
         at0 = core == 0
-        for u in range(UNROLL):
+        for u in us:
             g = step * UNROLL + u
             give_copy(g).wait_recv()
             full = jnp.exp(jnp.full((1, HEAD), -rate_of(mine + g) * rows, F32))
@@ -131,8 +131,8 @@
     def pairs(step):
         return [step * UNROLL + u for u in range(UNROLL)]
 
-    def both(step):
-        heads = [first + g for first in (mine, theirs) for g in pairs(step)]
+    def both(step, sides):
+        heads = [first + g for first in sides for g in pairs(step)]
         scores = [
             lax.dot_general(q[:, columns(h)], k[:, columns(h)], (((1,), (1,)), ((), ())), preferred_element_type=F32)
             for h in heads
@@ -144,8 +144,8 @@
         for x, h in zip(sums, heads):
             raw[:, columns(h)] = x
 
-    def output(step):
-        for first, ref in ((mine, low), (theirs, pass_in)):
+    def output(step, own_side):
+        for first, ref in [(mine, low)] if own_side else [(theirs, pass_in)]:
             heads = [first + g for g in pairs(step)]
             if ref is pass_in:
                 for g in pairs(step):
@@ -197,28 +197,38 @@
 
     @pl.when(chip >= 2)
     def _():
-        lax.fori_loop(0, STEPS, lambda step, _: (both(step), 0)[1], 0)
+        lax.fori_loop(0, STEPS, lambda step, _: (both(step, (mine, theirs)), 0)[1], 0)
 
     def step_c(step, _):
-        @pl.when((step < STEPS) & (chip > 0))
-        def _():
-            chain(step, False)
-
-        @pl.when((step < STEPS) & (chip < 2))
-        def _():
-            both(step)
-
-        @pl.when((step >= 1) & (chip != 1))
-        def _():
-            output(step - 1)
+        for u, side in enumerate((mine, theirs)):
+            @pl.when(chip > 0)
+            def _():
+                chain(step, False, (u,))
+
+            @pl.when(chip < 2)
+            def _():
+                both(step, (side,))
+
+            if u == 0:
+                @pl.when((step >= 1) & (chip != 1))
+                def _():
+                    output(step - 1, False)
+            else:
+                @pl.when(chip != 1)
+                def _():
+                    output(step, True)
 
         return 0
 
-    lax.fori_loop(0, STEPS + 1, step_c, 0)
+    lax.fori_loop(0, STEPS, step_c, 0)
+
+    @pl.when(chip != 1)
+    def _():
+        output(STEPS - 1, False)
 
     @pl.when(chip == 1)
     def _():
-        lax.fori_loop(0, STEPS, lambda step, _: (output(step), 0)[1], 0)
+        lax.fori_loop(0, STEPS, lambda step, _: (output(step, True), output(step, False), 0)[2], 0)
 
     flag_copy.wait_send()
 

time: 24.2 us -> 24.4 us (level)
  no operation moved by 1% of the time
where the time goes in v5:
time: 24.4 us; the launch traced here: 24.2 us
  Pallas kernels  23.4 us (96%)
  local copies, waits for them, and re-layouts  0.8 us (3%)
    pallas_call x1, Pallas kernels, on_device(): pl.pallas_call(functools.partial(kernel, chips), out_shape=jax.ShapeDtype...  23.4 us
    unnamed x1, local copies, waits for them, and re-layouts  0.8 us

profile of v5, /device:TPU:31, one launch (start us, length us, event | category | flops | bytes accessed | tf_op | source)
XLA Modules:
  0.0 24.2 jit_solution(15668900097797240670)
XLA Ops:
  0.0 23.4 %chain.1 = bf16[64,4096]{1,0:T(8,128)(2,1)S(1)} custom-call(s32[32]{0:T(128)} %exps_hbm.1, s32[1,64]{1,0:T(1,128)} %bitcast.3, f32[32,128]{1,0:T(8,128)} %bitcast.2, bf16[64,4096]{1,0:T(8,128)(2,1)} %q_hbm.1, bf16[64,4096]{1,0:T(8,128)(2,1)} %k_hbm.1, bf16[64,4096]{1,0:T(8,128)(2,1)} %v_hbm.1), custom_call_target="tpu_custom_call" | custom-call | tf_op jit(solution)/shard_map/chain/pallas_call | solution.py:255
  23.4 0.8 %copy.8 = bf16[64,4096]{1,0:T(8,128)(2,1)} copy(bf16[64,4096]{1,0:T(8,128)(2,1)S(1)} %chain.1) | data formatting | bytes 1048576

commit v6 on v4

--- a/solution.py
+++ b/solution.py
@@ -10,7 +10,7 @@
 HEADS = 32
 HEAD = 128
 HALF = HEADS // 2
-UNROLL = 2
+UNROLL = 4
 STEPS = HALF // UNROLL
 PIECES = 2
 PIECE = HEAD // PIECES

time: 24.2 us -> 23.9 us (0.988)
  Pallas kernels: 23.3 us -> 23 us
    pallas_call x1, Pallas kernels: 23.3 us -> 23 us  [on_device(): pl.pallas_call(functools.partial(kernel, chips), out_shape=jax.ShapeDtype...]
where the time goes in v6:
time: 23.9 us; the launch traced here: 23.8 us
  Pallas kernels  23 us (96%)
  local copies, waits for them, and re-layouts  0.8 us (3%)
    pallas_call x1, Pallas kernels, on_device(): pl.pallas_call(functools.partial(kernel, chips), out_shape=jax.ShapeDtype...  23 us
    unnamed x1, local copies, waits for them, and re-layouts  0.8 us

profile of v6, /device:TPU:31, one launch (start us, length us, event | category | flops | bytes accessed | tf_op | source)
XLA Modules:
  0.0 23.8 jit_solution(8927612787376628246)
XLA Ops:
  0.0 23.0 %chain.1 = bf16[64,4096]{1,0:T(8,128)(2,1)S(1)} custom-call(s32[32]{0:T(128)} %exps_hbm.1, s32[1,64]{1,0:T(1,128)} %bitcast.3, f32[32,128]{1,0:T(8,128)} %bitcast.2, bf16[64,4096]{1,0:T(8,128)(2,1)} %q_hbm.1, bf16[64,4096]{1,0:T(8,128)(2,1)} %k_hbm.1, bf16[64,4096]{1,0:T(8,128)(2,1)} %v_hbm.1), custom_call_target="tpu_custom_call" | custom-call | tf_op jit(solution)/shard_map/chain/pallas_call | solution.py:245
  23.0 0.8 %copy.8 = bf16[64,4096]{1,0:T(8,128)(2,1)} copy(bf16[64,4096]{1,0:T(8,128)(2,1)S(1)} %chain.1) | data formatting | bytes 1048576
